TPU v7x, 128 devices: a whole 4x4x4 slice. The times are simulated.
128 devices in a mesh: row: 8 (over x, core), col: 16 (over y, z).
Axes of the slice: x: 4, y: 4, z: 4, core: 2. Of those that a mesh axis runs over, the one named last changes fastest.
Arguments:
- features: bfloat16 [131072, 128], P(('row', 'col')), may hold values from -6 to 6
- weight: bfloat16 [128, 128], replicated, may hold values from -0.5 to 0.5
- bias_vector: float32 [128], replicated, may hold values from -3 to 3
- stripe_values: bfloat16 [131072, 8192], P(('row', 'col')), may hold values from -0.0625 to 0.0625
- tile_values: bfloat16 [4096, 128, 128], P(('row', 'col')), may hold values from -0.25 to 0.25
- tile_rows: int32 [4096], P(('row', 'col')), may hold values from 0 to 7
- tile_slots: int32 [4096], P(('row', 'col')), may hold values from 0 to 15
- send_lists: int32 [8, 16, 16, 1], P('row', 'col'), may hold values from 0 to 7
- cotangent: bfloat16 [131072, 128], P(('row', 'col')), may hold values from -6 to 6
Outputs:
- hidden_out: bfloat16 [131072, 128], P(('row', 'col'))
- grad_features: bfloat16 [131072, 128], P(('row', 'col'))
- grad_weight: float32 [128, 128], replicated
- grad_bias: float32 [128], replicated
All inputs are finite; a program needn't handle non-finite values.
Results may differ from a plain program's by a relative error of at most 0.02.
Values may be sent and summed in bfloat16 or wider, within the bound.
A program may use at most 128 MiB of HBM per device.

v0:
```python
import functools
import math

import jax
import jax.numpy as jnp
from jax import lax
from jax.experimental import pallas as pl
from jax.experimental.pallas import tpu as pltpu
from jax.sharding import PartitionSpec as P

MESH = pl.DeviceIdType.MESH
BF16 = jnp.bfloat16
F32 = jnp.float32
AG = 4
RS = 4


def mm(a, b):
    return jnp.dot(a, b, preferred_element_type=F32)


def order(read, n, lanes=128):
    sub = lax.broadcasted_iota(jnp.int32, (n, lanes), 0)
    lane = lax.broadcasted_iota(jnp.int32, (n, lanes), 1)
    col = jnp.zeros((n, lanes), jnp.int32)
    row = jnp.full((n, lanes), 1 << 20, jnp.int32)

    def one(t, both):
        v = read(t)
        return jnp.where(sub == t, v, both[0]), jnp.where(lane == t, v * n + t, both[1])

    col, row = lax.fori_loop(0, n, one, (col, row))
    less = (row < col * n + sub).astype(jnp.int32)
    rank = jnp.sum(less, axis=1, keepdims=True)
    hit = rank == lane
    perm = jnp.sum(jnp.where(hit, sub, 0), axis=0, keepdims=True)
    value = jnp.sum(jnp.where(hit, col, 0), axis=0, keepdims=True)
    last = jnp.sum((col <= lane).astype(jnp.int32), axis=0, keepdims=True)
    count = jnp.sum((col == lane).astype(jnp.int32), axis=0, keepdims=True)
    last = jnp.where(count > 0, last, 0)
    before = jnp.sum(((row // n == col) & (lane < sub)).astype(jnp.int32), axis=1, keepdims=True)
    again = jnp.sum(jnp.where(hit & (before > 0), 1, 0), axis=0, keepdims=True)
    return jnp.concatenate([perm, value, last, again] + [jnp.zeros_like(perm)] * 4, axis=0)


def kernel(
    nrow, ncol, scale,
    feat, weight, bias, stripe, tiles, rows_s, slots_s, lists_s, cot,
    hid_out, gf_out, gw_out, gb_out,
    st, fo, fg, tv, cv, recv, stage, meta_v, meta_s, scan, y, yb, gp, hid, gt, gtb,
    pa, ps, sr, xs, ra, rb, bst, brecv, gws, gwr, g2s, g2r, gwo, gfv, biasp,
    lsem, ssem, rsem, fsem, frsem, bsem, brsem, heard, a1s, a1r, a2s, a2r, a3s, a3r,
):
    nblk, blk, _ = feat.shape
    nt = tv.shape[0]
    nodes = nblk * blk
    r = lax.axis_index("row")
    c = lax.axis_index("col")
    chip, core = r // 2, r % 2
    chips = nrow // 2
    chip_r, chip_l, chip_f = (chip + 1) % chips, (chip + chips - 1) % chips, (chip + 2) % chips
    sib = chip * 2 + 1 - core
    right, left = chip_r * 2 + core, chip_l * 2 + core
    order_of = [
        chip * 2 + core, chip * 2 + 1 - core,
        chip_l * 2 + core, chip_l * 2 + 1 - core,
        chip_r * 2 + core, chip_r * 2 + 1 - core,
        chip_f * 2 + core, chip_f * 2 + 1 - core,
    ]

    def peer(d):
        return lax.rem(c + d, ncol)

    local = [
        pltpu.make_async_copy(feat, fo, lsem.at[8]),
        pltpu.make_async_copy(cot, cv, lsem.at[9]),
        pltpu.make_async_copy(tiles, tv, lsem.at[10]),
    ]
    local[0].start()
    stripes = [
        pltpu.make_async_copy(
            stripe.at[:, pl.ds(pl.multiple_of(order_of[k] * nodes, 128), nodes)], st.at[k], lsem.at[k]
        )
        for k in range(8)
    ]
    stripes[0].start()
    stripes[1].start()
    for k in range(2, 8):
        stripes[k].start()
    local[2].start()
    local[1].start()
    barrier = pltpu.get_barrier_semaphore()

    side = next(k for k in range(1, ncol + 1) if k * k >= ncol)
    cy, cz = c // side, c % side
    others = [(row, c) for row in (sib, right, left)]
    z_peers = [(r, cy * side + (cz + d) % side) for d in range(1, side)]
    y_peers = [(r, (cy + d) % (ncol // side) * side + cz) for d in range(1, ncol // side)]
    for dev in others + z_peers + y_peers:
        pl.semaphore_signal(barrier, inc=1, device_id=dev, device_id_type=MESH)

    meta_v[0:8] = order(lambda t: rows_s[t], nt)
    meta_v[8:16] = order(lambda t: lax.rem(c + ncol - slots_s[t], ncol), nt)
    meta_v[16:24] = order(lambda d: lists_s[peer(d)], ncol)
    meta_copy = pltpu.make_async_copy(meta_v, meta_s, lsem.at[11])
    meta_copy.start()

    pl.semaphore_wait(barrier, len(others + z_peers + y_peers))
    for dev in z_peers:
        pl.semaphore_signal(heard, inc=1, device_id=dev, device_id_type=MESH)

    piece, half = nodes // AG, AG // 2
    pb = piece // blk
    width, rhalf = nodes // RS, RS // 2

    def remote(i, src, dst, row):
        return pltpu.make_async_remote_copy(
            src_ref=src, dst_ref=dst, send_sem=ssem.at[i], recv_sem=rsem.at[i],
            device_id=(row, c), device_id_type=MESH,
        )

    def part(slot, p):
        own = fo if slot == 0 else fg.at[slot - 1]
        return own.at[pl.ds(p * pb, pb)]

    def own_right(p):
        return remote(p, part(0, p), part(2, p), right)

    def own_left(p):
        return remote(AG + p, part(0, p), part(4, p), left)

    def on_right(p):
        return remote(2 * AG + p, part(2, p), part(6, p), right)

    def on_left(p):
        return remote(2 * AG + p, part(4, p), part(6, p), left)

    def to_twin(slot, p):
        return remote(3 * AG + (slot - 2) // 2 * AG + p, part(slot, p), part(slot + 1, p), sib)

    own_twin = remote(6 * AG, fo, fg.at[0], sib)
    base = 6 * AG + 1

    def give(q, p):
        return remote(base + q * RS + p, ps.at[q, p], sr.at[q, p], sib)

    def first_right(p):
        return remote(base + 4 * RS + p, xs.at[2, p], ra.at[p], right)

    def first_left(p):
        return remote(base + 4 * RS + p, xs.at[2, p], ra.at[p], left)

    def last_right(p):
        return remote(base + 5 * RS + p, xs.at[1, p], rb.at[1, p], right)

    def last_left(p):
        return remote(base + 6 * RS + p, xs.at[0, p], rb.at[0, p], left)

    def loop(start, stop, act):
        def one(d, _):
            act(d)
            return 0

        lax.fori_loop(start, stop, one, 0)

    local[0].wait()
    own_right(0).start()
    own_left(AG - 1).start()
    own_twin.start()

    def own(i):
        own_right(i).start()
        own_left(AG - 1 - i).start()

    loop(1, AG, own)
    def block_copy(d):
        return pltpu.make_async_remote_copy(
            src_ref=stage.at[d], dst_ref=recv.at[d], send_sem=fsem.at[d], recv_sem=frsem.at[d],
            device_id=(r, peer(d)), device_id_type=MESH,
        )

    def picked(d):
        return fo[lists_s[peer(d)]]

    def send_block(d):
        stage[d] = picked(d)
        block_copy(d).start()

    def send_blocks():
        pl.semaphore_wait(heard, len(z_peers))
        recv[0] = picked(0)
        loop(1, ncol, send_block)

    def dense_all(slot, fresh):
        rows = nodes // 2
        src = fo if slot == 0 else fg.at[slot - 1]

        def one(i):
            at = pl.ds(pl.multiple_of(i * rows, rows), rows)
            v = mm(st[slot, at, :], src[...].reshape(nodes, -1))
            y[at, :] = v if fresh else y[at, :] + v

        loop(0, 2, one)

    stripes[0].wait()
    dense_all(0, True)
    stripes[1].wait()
    own_twin.wait_recv()
    dense_all(1, False)
    scan[0] = jnp.zeros((blk, blk), F32)

    def same(row, j):
        return meta_s[row, j].astype(F32)

    unroll = 4

    def scan_loop(n, row, term):
        def step(i):
            terms = [term(i * unroll + u) for u in range(unroll)]
            run_sum = scan[i * unroll]
            for u in range(unroll):
                run_sum = terms[u] + same(row, i * unroll + u) * run_sum
                scan[i * unroll + u + 1] = run_sum

        loop(0, n // unroll, step)

    def sparse_forward():
        meta_copy.wait()
        local[2].wait()

        def wait_block(d, _):
            block_copy(d).wait_recv()
            return 0

        lax.fori_loop(1, ncol, wait_block, 0)

        def product(j):
            t = meta_s[0, j]
            return mm(tv[t], recv[lax.rem(c + ncol - slots_s[t], ncol)])

        scan_loop(nt, 3, product)

        def put(k):
            y[pl.ds(pl.multiple_of(k * blk, blk), blk), :] += scan[meta_s[2, k]]

        loop(0, nblk, put)

    def add(one, p, two, q):
        rows = nodes // 2

        def half_rows(i):
            at = pl.ds(pl.multiple_of(i * rows, rows), rows)
            parts = [
                mm(st[slot, at, u * piece:(u + 1) * piece], fg[slot - 1, u * pb:(u + 1) * pb].reshape(piece, -1))
                for slot, u in ((one, p), (two, q))
            ]
            y[at, :] += parts[0] + parts[1]

        loop(0, 2, half_rows)

    def arrive(i):
        j = AG - 1 - i
        own_right(i).wait_recv()
        if i < half:
            on_right(i).start()
        to_twin(2, i).start()
        own_left(j).wait_recv()
        if i < half:
            on_left(j).start()
        to_twin(4, j).start()

    def twins(i):
        j = AG - 1 - i
        to_twin(2, i).wait_recv()
        to_twin(4, j).wait_recv()
        add(3, i, 5, j)

    def arrive_far(i):
        j = AG - 1 - i
        on_right(i).wait_recv()
        to_twin(6, i).start()
        on_left(j).wait_recv()
        to_twin(6, j).start()

    def far_twins(i):
        j = AG - 1 - i
        to_twin(6, i).wait_recv()
        to_twin(6, j).wait_recv()
        add(7, i, 7, j)

    for i in range(AG):
        arrive(i)
        if i == 0:
            send_blocks()
            stripes[2].wait()
            stripes[4].wait()
        add(2, i, 4, AG - 1 - i)
        if i == 0:
            stripes[3].wait()
            stripes[5].wait()
        else:
            twins(i - 1)
    twins(AG - 1)
    stripes[6].wait()
    stripes[7].wait()
    for i in range(half):
        arrive_far(i)
        add(6, i, 6, AG - 1 - i)
        if i == 0:
            sparse_forward()
        else:
            far_twins(i - 1)
    far_twins(half - 1)

    local[1].wait()
    w = weight[...]
    chunk = 4 * blk
    biasp[...] = jnp.zeros_like(biasp)

    def pointwise(k):
        s = pl.ds(pl.multiple_of(k * chunk, chunk), chunk)
        yk = y[s, :].astype(BF16)
        yb[s, :] = yk
        x = mm(yk, w) + bias[...]
        g = jax.nn.sigmoid(x)
        hid[s, :] = (x * g).astype(BF16)
        gk = (cv[s, :].astype(F32) * (g * (1.0 + x * (1.0 - g)))).astype(BF16)
        gp[s, :] = gk
        biasp[...] += jnp.sum(gk.astype(F32).reshape(chunk // 8, 8, blk), axis=0)
        gtk = lax.dot_general(w, gk, (((1,), (1,)), ((), ())), preferred_element_type=F32).astype(BF16)
        gt[:, s] = gtk
        for h in range(4):
            gtb[4 * k + h] = gtk[:, h * blk:(h + 1) * blk]

    loop(0, nodes // chunk, pointwise)
    hid_copy = pltpu.make_async_copy(hid, hid_out, lsem.at[12])
    hid_copy.start()

    group = min(2, RS)

    def back(slot, i):
        wide = group * width
        return mm(gt[...], st[slot, :, pl.ds(pl.multiple_of(i * wide, wide), wide)])

    def send_sib(q):
        def one(i):
            v = back(2 * q + 1, i).astype(BF16)
            for u in range(group):
                ps[q, i * group + u] = v[:, u * width:(u + 1) * width]
                give(q, i * group + u).start()

        loop(0, RS // group, one)

    def keep_own(q):
        def one(i):
            v = back(2 * q, i)
            for u in range(group):
                pa[q, i * group + u] = v[:, u * width:(u + 1) * width]

        loop(0, RS // group, one)

    def summed(q, p):
        give(q, p).wait_recv()
        return pa[q, p] + sr[q, p].astype(F32)

    send_sib(3)

    gw = lax.dot_general(yb[...], gp[...], (((0,), (0,)), ((), ())), preferred_element_type=F32)
    wrows = blk // ncol
    for q in range(ncol):
        gws[q, 0:wrows] = gw[q * wrows:(q + 1) * wrows, :]
        gws[q, wrows:wrows + 8] = biasp[...]

    def a1(d):
        return pltpu.make_async_remote_copy(
            src_ref=gws.at[peer(d)], dst_ref=gwr.at[d], send_sem=a1s.at[d], recv_sem=a1r.at[d],
            device_id=(r, peer(d)), device_id_type=MESH,
        )

    def a2(d):
        return pltpu.make_async_remote_copy(
            src_ref=g2s, dst_ref=g2r.at[d], send_sem=a2s.at[d], recv_sem=a2r.at[d],
            device_id=(lax.rem(r + d, nrow), c), device_id_type=MESH,
        )

    def a3(d, owner):
        return pltpu.make_async_remote_copy(
            src_ref=gwo.at[owner], dst_ref=gwo.at[owner], send_sem=a3s.at[d], recv_sem=a3r.at[d],
            device_id=(r, peer(d)), device_id_type=MESH,
        )

    def run(n, act):
        loop(1, n, act)

    run(ncol, lambda d: a1(d).start())

    keep_own(3)

    def first(i):
        j = RS - 1 - i
        xs[2, i] = summed(3, i).astype(BF16)
        first_right(i).start()
        xs[2, j] = summed(3, j).astype(BF16)
        first_left(j).start()

    loop(0, rhalf, first)

    def back_copy(d):
        return pltpu.make_async_remote_copy(
            src_ref=bst.at[d], dst_ref=brecv.at[d], send_sem=bsem.at[d], recv_sem=brsem.at[d],
            device_id=(r, lax.rem(c + ncol - d, ncol)), device_id_type=MESH,
        )

    def bproduct(j):
        t = meta_s[8, j]
        return mm(gtb[rows_s[t]], tv[t])

    scan_loop(nt, 11, bproduct)

    def slot_sum(d):
        return scan[meta_s[10, d]].astype(BF16)

    brecv[0] = slot_sum(0)

    def send_back(d, _):
        bst[d] = slot_sum(d)
        back_copy(d).start()
        return 0

    lax.fori_loop(1, ncol, send_back, 0)

    send_sib(2)
    send_sib(1)
    keep_own(2)
    keep_own(1)

    def direct(i):
        j = RS - 1 - i
        xs[1, j] = summed(2, j).astype(BF16)
        last_right(j).start()
        xs[0, i] = summed(1, i).astype(BF16)
        last_left(i).start()

    loop(0, rhalf, direct)
    run(ncol, lambda d: a1(d).wait_recv())
    part2 = gws[c]
    for d in range(1, ncol):
        part2 += gwr[d]
    g2s[...] = part2
    run(nrow, lambda d: a2(d).start())

    send_sib(0)
    keep_own(0)

    def relay(i):
        j = RS - 1 - i
        first_right(i).wait_recv()
        xs[1, i] = (summed(2, i) + ra[i].astype(F32)).astype(BF16)
        last_right(i).start()
        first_left(j).wait_recv()
        xs[0, j] = (summed(1, j) + ra[j].astype(F32)).astype(BF16)
        last_left(j).start()

    loop(0, rhalf, relay)

    run(nrow, lambda d: a2(d).wait_recv())
    part3 = g2s[...]
    for d in range(1, nrow):
        part3 += g2r[d]
    gwo[c] = part3[0:wrows] * scale
    gb_out[...] = jnp.sum(part3[wrows:wrows + 8], axis=0, keepdims=True) * scale
    run(ncol, lambda d: a3(d, c).start())

    run(ncol, lambda d: back_copy(d).wait_recv())

    scan_loop(ncol, 19, lambda j: brecv[meta_s[16, j]].astype(F32))

    per = width // blk

    def gf_copy(p):
        s = pl.ds(pl.multiple_of(p * width, width), width)
        return pltpu.make_async_copy(gfv.at[s], gf_out.at[s], lsem.at[13 + p])

    def finish(p):
        total = summed(0, p)
        last_right(p).wait_recv()
        last_left(p).wait_recv()
        total = total + rb[0, p].astype(F32) + rb[1, p].astype(F32)
        for h in range(per):
            k = p * per + h
            block = total[:, h * blk:(h + 1) * blk] + scan[meta_s[18, k]]
            gfv[pl.ds(pl.multiple_of(k * blk, blk), blk), :] = block.T.astype(BF16)
        gf_copy(p).start()

    for i in range(rhalf):
        finish(i)
        finish(RS - 1 - i)

    run(ncol, lambda d: a3(d, lax.rem(c + ncol - d, ncol)).wait_recv())
    gw_out[...] = gwo[...].reshape(gw_out.shape)

    def ag_sent(p):
        own_right(p).wait_send()
        own_left(p).wait_send()
        for slot in (2, 4, 6):
            to_twin(slot, p).wait_send()
        on_right(p).wait_send()

    own_twin.wait_send()
    loop(0, AG, ag_sent)

    def rs_sent(p):
        for q in range(4):
            give(q, p).wait_send()
        first_right(p).wait_send()
        last_right(p).wait_send()
        last_left(p).wait_send()

    loop(0, RS, rs_sent)
    run(ncol, lambda d: block_copy(d).wait_send())
    run(ncol, lambda d: back_copy(d).wait_send())
    run(ncol, lambda d: a1(d).wait_send())
    run(nrow, lambda d: a2(d).wait_send())
    run(ncol, lambda d: a3(d, c).wait_send())
    hid_copy.wait()
    loop(0, RS, lambda p: gf_copy(p).wait())


def hand_over(*refs):
    sems = refs[-1]
    copies = [pltpu.make_async_copy(refs[i], refs[4 + i], sems.at[i]) for i in range(4)]
    for copy in copies:
        copy.start()
    for copy in copies:
        copy.wait()


def solution(mesh):
    nrow, ncol = mesh.shape["row"], mesh.shape["col"]

    def body(features, weight, bias_vector, stripe_values, tile_values, tile_rows, tile_slots, send_lists, cotangent):
        nodes, f = features.shape
        nt, blk, _ = tile_values.shape
        nblk = nodes // blk
        wrows = blk // ncol
        scale = 1.0 / math.sqrt(nodes * nrow * ncol)
        vm = pltpu.VMEM
        dma = pltpu.SemaphoreType.DMA
        copies = 6 * AG + 1 + 7 * RS
        any_, vmem, smem = (pl.BlockSpec(memory_space=m) for m in (pl.ANY, pltpu.VMEM, pltpu.SMEM))
        shapes = (
            jax.ShapeDtypeStruct((nodes, f), BF16),
            jax.ShapeDtypeStruct((nodes, f), BF16),
            jax.ShapeDtypeStruct((f, f), F32),
            jax.ShapeDtypeStruct((1, f), F32),
        )
        made = pl.pallas_call(
            functools.partial(kernel, nrow, ncol, scale),
            out_shape=shapes,
            in_specs=[any_, vmem, vmem, any_, any_, smem, smem, smem, any_],
            out_specs=(any_, any_, vmem, vmem),
            scratch_shapes=[
                vm((8, nodes, nodes), BF16),
                vm((nblk, blk, f), BF16),
                vm((7, nblk, blk, f), BF16),
                vm((nt, blk, blk), BF16),
                vm((nodes, f), BF16),
                vm((ncol, blk, f), BF16),
                vm((ncol, blk, f), BF16),
                vm((24, 128), jnp.int32),
                pltpu.SMEM((24, 128), jnp.int32),
                vm((nt + 1, blk, blk), F32),
                vm((nodes, f), F32),
                vm((nodes, f), BF16),
                vm((nodes, f), BF16),
                vm((nodes, f), BF16),
                vm((f, nodes), BF16),
                vm((nblk, f, blk), BF16),
                vm((4, RS, f, nodes // RS), F32),
                vm((4, RS, f, nodes // RS), BF16),
                vm((4, RS, f, nodes // RS), BF16),
                vm((3, RS, f, nodes // RS), BF16),
                vm((RS, f, nodes // RS), BF16),
                vm((2, RS, f, nodes // RS), BF16),
                vm((ncol, f, blk), BF16),
                vm((ncol, f, blk), BF16),
                vm((ncol, wrows + 8, f), F32),
                vm((ncol, wrows + 8, f), F32),
                vm((wrows + 8, f), F32),
                vm((nrow, wrows + 8, f), F32),
                vm((ncol, wrows, f), F32),
                vm((nodes, f), BF16),
                vm((8, f), F32),
                dma((13 + RS,)),
                dma((copies,)), dma((copies,)),
                dma((ncol,)), dma((ncol,)), dma((ncol,)), dma((ncol,)),
                pltpu.SemaphoreType.REGULAR,
                dma((ncol,)), dma((ncol,)), dma((nrow,)), dma((nrow,)), dma((ncol,)), dma((ncol,)),
            ],
            compiler_params=pltpu.CompilerParams(
                collective_id=0, has_side_effects=True, vmem_limit_bytes=56 * 2**20
            ),
        )(
            features.reshape(nblk, blk, f), weight, bias_vector.reshape(1, f), stripe_values, tile_values,
            tile_rows, tile_slots, send_lists.reshape(ncol), cotangent,
        )
        hid, gf, gw, gb = pl.pallas_call(
            hand_over, out_shape=shapes, in_specs=[vmem] * 4, out_specs=(any_,) * 4, scratch_shapes=[dma((4,))]
        )(*made)
        return hid, gf, gw, gb.reshape(f)

    return jax.shard_map(
        body,
        mesh=mesh,
        in_specs=(
            P(("row", "col"), None),
            P(),
            P(),
            P(("row", "col"), None),
            P(("row", "col"), None, None),
            P(("row", "col")),
            P(("row", "col")),
            P("row", "col", None, None),
            P(("row", "col"), None),
        ),
        out_specs=(P(("row", "col"), None), P(("row", "col"), None), P(), P()),
        check_vma=False,
    )
```

profile of v0, /device:TPU:1, one launch (start us, length us, event | category | flops | bytes accessed | tf_op | source)
XLA Modules:
  0.0 47.7 jit_solution(11813546115493518752)
XLA Ops:
  0.6 45.2 %shard_map.120 = (bf16[1024,128]{1,0:T(8,128)(2,1)}, bf16[1024,128]{1,0:T(8,128)(2,1)}, f32[128,128]{1,0:T(8,128)}, f32[1,128]{1,0:T(1,128)}) custom-call(bf16[8,128,128]{2,1,0:T(8,128)(2,1)} %bitcast.4, bf16[128,128]{1,0:T(8,128)(2,1)} %weight.1, f32[1,128]{1,0:T(1,128)} %bitcast.5, bf16[1024,8192]{1,0:T(8,128)(2,1)} %stripe.1, ...), custom_call_target="tpu_custom_call" | custom-call | tf_op jit(solution)/shard_map/pallas_call | solution.py:557
  45.8 1.9 %shard_map.121 = (bf16[1024,128]{1,0:T(8,128)(2,1)}, bf16[1024,128]{1,0:T(8,128)(2,1)}, f32[128,128]{1,0:T(8,128)}, f32[1,128]{1,0:T(1,128)}) custom-call(bf16[1024,128]{1,0:T(8,128)(2,1)} %get-tuple-element.12.refs_0_, bf16[1024,128]{1,0:T(8,128)(2,1)} %get-tuple-element.13.refs_1_, f32[128,128]{1,0:T(8,128)} %get-tuple-element.14.refs_2_, ...), custom_call_target="tpu_custom_call" | custom-call | tf_op jit(solution)/shard_map/pallas_call | solution.py:607
where the time goes:
time: 47.9 us; the launch traced here: 47.7 us
  Pallas kernels  47 us (98%)
  between operations  0.64 us (1%)
    pallas_call x1, Pallas kernels, body(): pl.pallas_call(functools.partial(kernel, nrow, ncol, scale), out_shape=sh...  45.2 us
    pallas_call x1, Pallas kernels, body(): pl.pallas_call(hand_over, out_shape=shapes, in_specs=[vmem] * 4, out_spec...  1.87 us

commit v1 on v0

--- a/solution.py
+++ b/solution.py
@@ -11,8 +11,8 @@
 MESH = pl.DeviceIdType.MESH
 BF16 = jnp.bfloat16
 F32 = jnp.float32
-AG = 4
-RS = 4
+AG = 2
+RS = 2
 
 
 def mm(a, b):
@@ -49,7 +49,7 @@
     hid_out, gf_out, gw_out, gb_out,
     st, fo, fg, tv, cv, recv, stage, meta_v, meta_s, scan, y, yb, gp, hid, gt, gtb,
     pa, ps, sr, xs, ra, rb, bst, brecv, gws, gwr, g2s, g2r, gwo, gfv, biasp,
-    lsem, ssem, rsem, fsem, frsem, bsem, brsem, heard, a1s, a1r, a2s, a2r, a3s, a3r,
+    lsem, rsem, fsem, frsem, bsem, brsem, gsem, tsem, heard, a1s, a1r, a2s, a2r, a3s, a3r,
 ):
     nblk, blk, _ = feat.shape
     nt = tv.shape[0]
@@ -68,8 +68,18 @@
         chip_f * 2 + core, chip_f * 2 + 1 - core,
     ]
 
+    side = next(k for k in range(1, ncol + 1) if k * k >= ncol)
+    lines = ncol // side
+    cy, cz = c // side, c % side
+
     def peer(d):
-        return lax.rem(c + d, ncol)
+        return lax.rem(cy + d // side, lines) * side + lax.rem(cz + d % side, side)
+
+    def back_peer(d):
+        return lax.rem(cy + lines - d // side, lines) * side + lax.rem(cz + side - d % side, side)
+
+    def offset(q):
+        return lax.rem(cy + lines - q // side, lines) * side + lax.rem(cz + side - q % side, side)
 
     local = [
         pltpu.make_async_copy(feat, fo, lsem.at[8]),
@@ -91,16 +101,14 @@
     local[1].start()
     barrier = pltpu.get_barrier_semaphore()
 
-    side = next(k for k in range(1, ncol + 1) if k * k >= ncol)
-    cy, cz = c // side, c % side
     others = [(row, c) for row in (sib, right, left)]
     z_peers = [(r, cy * side + (cz + d) % side) for d in range(1, side)]
-    y_peers = [(r, (cy + d) % (ncol // side) * side + cz) for d in range(1, ncol // side)]
+    y_peers = [(r, (cy + d) % lines * side + cz) for d in range(1, lines)]
     for dev in others + z_peers + y_peers:
         pl.semaphore_signal(barrier, inc=1, device_id=dev, device_id_type=MESH)
 
     meta_v[0:8] = order(lambda t: rows_s[t], nt)
-    meta_v[8:16] = order(lambda t: lax.rem(c + ncol - slots_s[t], ncol), nt)
+    meta_v[8:16] = order(lambda t: offset(slots_s[t]), nt)
     meta_v[16:24] = order(lambda d: lists_s[peer(d)], ncol)
     meta_copy = pltpu.make_async_copy(meta_v, meta_s, lsem.at[11])
     meta_copy.start()
@@ -113,11 +121,20 @@
     pb = piece // blk
     width, rhalf = nodes // RS, RS // 2
 
-    def remote(i, src, dst, row):
+    def remote(i, src, dst, row, sent=gsem):
         return pltpu.make_async_remote_copy(
-            src_ref=src, dst_ref=dst, send_sem=ssem.at[i], recv_sem=rsem.at[i],
+            src_ref=src, dst_ref=dst, send_sem=sent, recv_sem=rsem.at[i],
             device_id=(row, c), device_id_type=MESH,
         )
+
+    def whole(ref, sent, received):
+        return pltpu.make_async_remote_copy(
+            src_ref=ref, dst_ref=ref, send_sem=sent, recv_sem=received,
+            device_id=(sib, c), device_id_type=MESH,
+        )
+
+    def after_first(ref, sent, received):
+        return whole(ref.at[pl.ds(1, ref.shape[0] - 1)], sent, received)
 
     def part(slot, p):
         own = fo if slot == 0 else fg.at[slot - 1]
@@ -142,19 +159,19 @@
     base = 6 * AG + 1
 
     def give(q, p):
-        return remote(base + q * RS + p, ps.at[q, p], sr.at[q, p], sib)
+        return remote(base + q * RS + p, ps.at[q, p], sr.at[q, p], sib, tsem)
 
     def first_right(p):
-        return remote(base + 4 * RS + p, xs.at[2, p], ra.at[p], right)
+        return remote(base + 4 * RS + p, xs.at[2, p], ra.at[p], right, tsem)
 
     def first_left(p):
-        return remote(base + 4 * RS + p, xs.at[2, p], ra.at[p], left)
+        return remote(base + 4 * RS + p, xs.at[2, p], ra.at[p], left, tsem)
 
     def last_right(p):
-        return remote(base + 5 * RS + p, xs.at[1, p], rb.at[1, p], right)
+        return remote(base + 5 * RS + p, xs.at[1, p], rb.at[1, p], right, tsem)
 
     def last_left(p):
-        return remote(base + 6 * RS + p, xs.at[0, p], rb.at[0, p], left)
+        return remote(base + 6 * RS + p, xs.at[0, p], rb.at[0, p], left, tsem)
 
     def loop(start, stop, act):
         def one(d, _):
@@ -175,7 +192,7 @@
     loop(1, AG, own)
     def block_copy(d):
         return pltpu.make_async_remote_copy(
-            src_ref=stage.at[d], dst_ref=recv.at[d], send_sem=fsem.at[d], recv_sem=frsem.at[d],
+            src_ref=stage.at[d], dst_ref=recv.at[d], send_sem=fsem, recv_sem=frsem,
             device_id=(r, peer(d)), device_id_type=MESH,
         )
 
@@ -188,8 +205,12 @@
 
     def send_blocks():
         pl.semaphore_wait(heard, len(z_peers))
-        recv[0] = picked(0)
-        loop(1, ncol, send_block)
+        for i in range(1, lines):
+            loop(i * side + 1, (i + 1) * side, send_block)
+
+    loop(1, side, send_block)
+    loop(1, lines, lambda i: send_block(i * side))
+    recv[0] = picked(0)
 
     def dense_all(slot, fresh):
         rows = nodes // 2
@@ -227,16 +248,11 @@
     def sparse_forward():
         meta_copy.wait()
         local[2].wait()
-
-        def wait_block(d, _):
-            block_copy(d).wait_recv()
-            return 0
-
-        lax.fori_loop(1, ncol, wait_block, 0)
+        after_first(recv, fsem, frsem).wait_recv()
 
         def product(j):
             t = meta_s[0, j]
-            return mm(tv[t], recv[lax.rem(c + ncol - slots_s[t], ncol)])
+            return mm(tv[t], recv[offset(slots_s[t])])
 
         scan_loop(nt, 3, product)
 
@@ -373,19 +389,19 @@
 
     def a1(d):
         return pltpu.make_async_remote_copy(
-            src_ref=gws.at[peer(d)], dst_ref=gwr.at[d], send_sem=a1s.at[d], recv_sem=a1r.at[d],
+            src_ref=gws.at[peer(d)], dst_ref=gwr.at[d], send_sem=a1s, recv_sem=a1r,
             device_id=(r, peer(d)), device_id_type=MESH,
         )
 
     def a2(d):
         return pltpu.make_async_remote_copy(
-            src_ref=g2s, dst_ref=g2r.at[d], send_sem=a2s.at[d], recv_sem=a2r.at[d],
+            src_ref=g2s, dst_ref=g2r.at[d], send_sem=a2s, recv_sem=a2r,
             device_id=(lax.rem(r + d, nrow), c), device_id_type=MESH,
         )
 
-    def a3(d, owner):
+    def a3(d):
         return pltpu.make_async_remote_copy(
-            src_ref=gwo.at[owner], dst_ref=gwo.at[owner], send_sem=a3s.at[d], recv_sem=a3r.at[d],
+            src_ref=gwo.at[0], dst_ref=gwo.at[d], send_sem=a3s, recv_sem=a3r,
             device_id=(r, peer(d)), device_id_type=MESH,
         )
 
@@ -407,8 +423,8 @@
 
     def back_copy(d):
         return pltpu.make_async_remote_copy(
-            src_ref=bst.at[d], dst_ref=brecv.at[d], send_sem=bsem.at[d], recv_sem=brsem.at[d],
-            device_id=(r, lax.rem(c + ncol - d, ncol)), device_id_type=MESH,
+            src_ref=bst.at[d], dst_ref=brecv.at[d], send_sem=bsem, recv_sem=brsem,
+            device_id=(r, back_peer(d)), device_id_type=MESH,
         )
 
     def bproduct(j):
@@ -433,6 +449,13 @@
     send_sib(1)
     keep_own(2)
     keep_own(1)
+    after_first(gwr, a1s, a1r).wait_recv()
+    part2 = gws[c]
+    for d in range(1, ncol):
+        part2 += gwr[d]
+    g2s[...] = part2
+    run(nrow, lambda d: a2(d).start())
+
 
     def direct(i):
         j = RS - 1 - i
@@ -442,13 +465,6 @@
         last_left(i).start()
 
     loop(0, rhalf, direct)
-    run(ncol, lambda d: a1(d).wait_recv())
-    part2 = gws[c]
-    for d in range(1, ncol):
-        part2 += gwr[d]
-    g2s[...] = part2
-    run(nrow, lambda d: a2(d).start())
-
     send_sib(0)
     keep_own(0)
 
@@ -461,17 +477,19 @@
         xs[0, j] = (summed(1, j) + ra[j].astype(F32)).astype(BF16)
         last_left(j).start()
 
+    whole(fg, gsem, gsem).wait_send()
+    after_first(stage, fsem, frsem).wait_send()
     loop(0, rhalf, relay)
 
-    run(nrow, lambda d: a2(d).wait_recv())
+    after_first(g2r, a2s, a2r).wait_recv()
     part3 = g2s[...]
     for d in range(1, nrow):
         part3 += g2r[d]
-    gwo[c] = part3[0:wrows] * scale
+    gwo[0] = part3[0:wrows] * scale
     gb_out[...] = jnp.sum(part3[wrows:wrows + 8], axis=0, keepdims=True) * scale
-    run(ncol, lambda d: a3(d, c).start())
-
-    run(ncol, lambda d: back_copy(d).wait_recv())
+    run(ncol, lambda d: a3(d).start())
+
+    after_first(brecv, bsem, brsem).wait_recv()
 
     scan_loop(ncol, 19, lambda j: brecv[meta_s[16, j]].astype(F32))
 
@@ -481,11 +499,14 @@
         s = pl.ds(pl.multiple_of(p * width, width), width)
         return pltpu.make_async_copy(gfv.at[s], gf_out.at[s], lsem.at[13 + p])
 
-    def finish(p):
+    def prepare(p, direct, from_side):
         total = summed(0, p)
-        last_right(p).wait_recv()
-        last_left(p).wait_recv()
-        total = total + rb[0, p].astype(F32) + rb[1, p].astype(F32)
+        direct(p).wait_recv()
+        pa[0, p] = total + rb[from_side, p].astype(F32)
+
+    def finish(p, relayed, from_side):
+        relayed(p).wait_recv()
+        total = pa[0, p] + rb[from_side, p].astype(F32)
         for h in range(per):
             k = p * per + h
             block = total[:, h * blk:(h + 1) * blk] + scan[meta_s[18, k]]
@@ -493,35 +514,24 @@
         gf_copy(p).start()
 
     for i in range(rhalf):
-        finish(i)
-        finish(RS - 1 - i)
-
-    run(ncol, lambda d: a3(d, lax.rem(c + ncol - d, ncol)).wait_recv())
-    gw_out[...] = gwo[...].reshape(gw_out.shape)
-
-    def ag_sent(p):
-        own_right(p).wait_send()
-        own_left(p).wait_send()
-        for slot in (2, 4, 6):
-            to_twin(slot, p).wait_send()
-        on_right(p).wait_send()
-
-    own_twin.wait_send()
-    loop(0, AG, ag_sent)
-
-    def rs_sent(p):
-        for q in range(4):
-            give(q, p).wait_send()
-        first_right(p).wait_send()
-        last_right(p).wait_send()
-        last_left(p).wait_send()
-
-    loop(0, RS, rs_sent)
-    run(ncol, lambda d: block_copy(d).wait_send())
-    run(ncol, lambda d: back_copy(d).wait_send())
-    run(ncol, lambda d: a1(d).wait_send())
-    run(nrow, lambda d: a2(d).wait_send())
-    run(ncol, lambda d: a3(d, c).wait_send())
+        prepare(i, last_left, 0)
+        prepare(RS - 1 - i, last_right, 1)
+    after_first(bst, bsem, brsem).wait_send()
+    after_first(gwr, a1s, a1r).wait_send()
+    after_first(g2r, a2s, a2r).wait_send()
+    for i in range(rhalf):
+        finish(i, last_right, 1)
+        finish(RS - 1 - i, last_left, 0)
+
+    after_first(gwo, a3s, a3r).wait_recv()
+
+    def place(d):
+        at = pl.multiple_of(back_peer(d) * wrows, wrows)
+        gw_out[pl.ds(at, wrows), :] = gwo[d]
+
+    loop(0, ncol, place)
+    after_first(gwo, a3s, a3r).wait_send()
+    whole(fg, tsem, tsem).wait_send()
     hid_copy.wait()
     loop(0, RS, lambda p: gf_copy(p).wait())
 
@@ -592,10 +602,10 @@
                 vm((nodes, f), BF16),
                 vm((8, f), F32),
                 dma((13 + RS,)),
-                dma((copies,)), dma((copies,)),
-                dma((ncol,)), dma((ncol,)), dma((ncol,)), dma((ncol,)),
+                dma((copies,)),
+                dma(()), dma(()), dma(()), dma(()), dma(()), dma(()),
                 pltpu.SemaphoreType.REGULAR,
-                dma((ncol,)), dma((ncol,)), dma((nrow,)), dma((nrow,)), dma((ncol,)), dma((ncol,)),
+                dma(()), dma(()), dma(()), dma(()), dma(()), dma(()),
             ],
             compiler_params=pltpu.CompilerParams(
                 collective_id=0, has_side_effects=True, vmem_limit_bytes=56 * 2**20

time: 47.9 us -> 42.5 us (0.89)
  Pallas kernels: 47 us -> 41.6 us
    pallas_call x1, Pallas kernels: 45.2 us -> 39.8 us  [body(): pl.pallas_call(functools.partial(kernel, nrow, ncol, scale), out_shape=sh...]
where the time goes in v1:
time: 42.5 us; the launch traced here: 42.3 us
  Pallas kernels  41.6 us (98%)
  between operations  0.64 us (2%)
    pallas_call x1, Pallas kernels, body(): pl.pallas_call(functools.partial(kernel, nrow, ncol, scale), out_shape=sh...  39.8 us
    pallas_call x1, Pallas kernels, body(): pl.pallas_call(hand_over, out_shape=shapes, in_specs=[vmem] * 4, out_spec...  1.87 us

profile of v1, /device:TPU:1, one launch (start us, length us, event | category | flops | bytes accessed | tf_op | source)
XLA Modules:
  0.0 42.3 jit_solution(14787020556791457936)
XLA Ops:
  0.6 39.8 %shard_map.120 = (bf16[1024,128]{1,0:T(8,128)(2,1)}, bf16[1024,128]{1,0:T(8,128)(2,1)}, f32[128,128]{1,0:T(8,128)}, f32[1,128]{1,0:T(1,128)}) custom-call(bf16[8,128,128]{2,1,0:T(8,128)(2,1)} %bitcast.4, bf16[128,128]{1,0:T(8,128)(2,1)} %weight.1, f32[1,128]{1,0:T(1,128)} %bitcast.5, bf16[1024,8192]{1,0:T(8,128)(2,1)} %stripe.1, ...), custom_call_target="tpu_custom_call" | custom-call | tf_op jit(solution)/shard_map/pallas_call | solution.py:567
  40.4 1.9 %shard_map.121 = (bf16[1024,128]{1,0:T(8,128)(2,1)}, bf16[1024,128]{1,0:T(8,128)(2,1)}, f32[128,128]{1,0:T(8,128)}, f32[1,128]{1,0:T(1,128)}) custom-call(bf16[1024,128]{1,0:T(8,128)(2,1)} %get-tuple-element.12.refs_0_, bf16[1024,128]{1,0:T(8,128)(2,1)} %get-tuple-element.13.refs_1_, f32[128,128]{1,0:T(8,128)} %get-tuple-element.14.refs_2_, ...), custom_call_target="tpu_custom_call" | custom-call | tf_op jit(solution)/shard_map/pallas_call | solution.py:617

commit v2 on v1

--- a/solution.py
+++ b/solution.py
@@ -45,15 +45,21 @@
 
 def kernel(
     nrow, ncol, scale,
-    feat, weight, bias, stripe, tiles, rows_s, slots_s, lists_s, cot,
+    feat, weight_h, bias_h, stripe, tiles, rows_h, slots_h, lists_h, cot,
     hid_out, gf_out, gw_out, gb_out,
-    st, fo, fg, tv, cv, recv, stage, meta_v, meta_s, scan, y, yb, gp, hid, gt, gtb,
+    weight, bias, rows_s, slots_s, lists_s, st, fo, fg, tv, cv, recv, stage, meta_v, meta_s, scan, y, yb, gp, hid, gt, gtb,
     pa, ps, sr, xs, ra, rb, bst, brecv, gws, gwr, g2s, g2r, gwo, gfv, biasp,
     lsem, rsem, fsem, frsem, bsem, brsem, gsem, tsem, heard, a1s, a1r, a2s, a2r, a3s, a3r,
 ):
     nblk, blk, _ = feat.shape
     nt = tv.shape[0]
     nodes = nblk * blk
+    small = [
+        pltpu.make_async_copy(x, y_, lsem.at[13 + RS + i])
+        for i, (x, y_) in enumerate(
+            [(rows_h, rows_s), (slots_h, slots_s), (lists_h, lists_s), (weight_h, weight), (bias_h, bias)]
+        )
+    ]
     r = lax.axis_index("row")
     c = lax.axis_index("col")
     chip, core = r // 2, r % 2
@@ -86,6 +92,16 @@
         pltpu.make_async_copy(cot, cv, lsem.at[9]),
         pltpu.make_async_copy(tiles, tv, lsem.at[10]),
     ]
+    barrier = pltpu.get_barrier_semaphore()
+
+    others = [(row, c) for row in (sib, right, left)]
+    z_peers = [(r, cy * side + (cz + d) % side) for d in range(1, side)]
+    y_peers = [(r, (cy + d) % lines * side + cz) for d in range(1, lines)]
+    for dev in others + z_peers + y_peers:
+        pl.semaphore_signal(barrier, inc=1, device_id=dev, device_id_type=MESH)
+
+    for copy in small:
+        copy.start()
     local[0].start()
     stripes = [
         pltpu.make_async_copy(
@@ -99,14 +115,8 @@
         stripes[k].start()
     local[2].start()
     local[1].start()
-    barrier = pltpu.get_barrier_semaphore()
-
-    others = [(row, c) for row in (sib, right, left)]
-    z_peers = [(r, cy * side + (cz + d) % side) for d in range(1, side)]
-    y_peers = [(r, (cy + d) % lines * side + cz) for d in range(1, lines)]
-    for dev in others + z_peers + y_peers:
-        pl.semaphore_signal(barrier, inc=1, device_id=dev, device_id_type=MESH)
-
+    for copy in small:
+        copy.wait()
     meta_v[0:8] = order(lambda t: rows_s[t], nt)
     meta_v[8:16] = order(lambda t: offset(slots_s[t]), nt)
     meta_v[16:24] = order(lambda d: lists_s[peer(d)], ncol)
@@ -304,10 +314,10 @@
         to_twin(6, j).wait_recv()
         add(7, i, 7, j)
 
+    send_blocks()
     for i in range(AG):
         arrive(i)
         if i == 0:
-            send_blocks()
             stripes[2].wait()
             stripes[4].wait()
         add(2, i, 4, AG - 1 - i)
@@ -330,7 +340,7 @@
 
     local[1].wait()
     w = weight[...]
-    chunk = 4 * blk
+    chunk = 8 * blk
     biasp[...] = jnp.zeros_like(biasp)
 
     def pointwise(k):
@@ -345,8 +355,8 @@
         biasp[...] += jnp.sum(gk.astype(F32).reshape(chunk // 8, 8, blk), axis=0)
         gtk = lax.dot_general(w, gk, (((1,), (1,)), ((), ())), preferred_element_type=F32).astype(BF16)
         gt[:, s] = gtk
-        for h in range(4):
-            gtb[4 * k + h] = gtk[:, h * blk:(h + 1) * blk]
+        for h in range(8):
+            gtb[8 * k + h] = gtk[:, h * blk:(h + 1) * blk]
 
     loop(0, nodes // chunk, pointwise)
     hid_copy = pltpu.make_async_copy(hid, hid_out, lsem.at[12])
@@ -567,9 +577,14 @@
         made = pl.pallas_call(
             functools.partial(kernel, nrow, ncol, scale),
             out_shape=shapes,
-            in_specs=[any_, vmem, vmem, any_, any_, smem, smem, smem, any_],
+            in_specs=[any_] * 9,
             out_specs=(any_, any_, vmem, vmem),
             scratch_shapes=[
+                vm((f, f), BF16),
+                vm((1, f), F32),
+                pltpu.SMEM((nt,), jnp.int32),
+                pltpu.SMEM((nt,), jnp.int32),
+                pltpu.SMEM((ncol,), jnp.int32),
                 vm((8, nodes, nodes), BF16),
                 vm((nblk, blk, f), BF16),
                 vm((7, nblk, blk, f), BF16),
@@ -601,7 +616,7 @@
                 vm((ncol, wrows, f), F32),
                 vm((nodes, f), BF16),
                 vm((8, f), F32),
-                dma((13 + RS,)),
+                dma((18 + RS,)),
                 dma((copies,)),
                 dma(()), dma(()), dma(()), dma(()), dma(()), dma(()),
                 pltpu.SemaphoreType.REGULAR,

time: 42.5 us -> 41.3 us (0.972)
  Pallas kernels: 41.6 us -> 40.5 us
    pallas_call x1, Pallas kernels: 39.8 us -> 38.7 us  [body(): pl.pallas_call(functools.partial(kernel, nrow, ncol, scale), out_shape=sh...]
where the time goes in v2:
time: 41.3 us; the launch traced here: 41.2 us
  Pallas kernels  40.5 us (98%)
  between operations  0.64 us (2%)
    pallas_call x1, Pallas kernels, body(): pl.pallas_call(functools.partial(kernel, nrow, ncol, scale), out_shape=sh...  38.7 us
    pallas_call x1, Pallas kernels, body(): pl.pallas_call(hand_over, out_shape=shapes, in_specs=[vmem] * 4, out_spec...  1.87 us

profile of v2, /device:TPU:1, one launch (start us, length us, event | category | flops | bytes accessed | tf_op | source)
XLA Modules:
  0.0 41.2 jit_solution(7295696060466554203)
XLA Ops:
  0.6 38.7 %shard_map.120 = (bf16[1024,128]{1,0:T(8,128)(2,1)}, bf16[1024,128]{1,0:T(8,128)(2,1)}, f32[128,128]{1,0:T(8,128)}, f32[1,128]{1,0:T(1,128)}) custom-call(bf16[8,128,128]{2,1,0:T(8,128)(2,1)} %bitcast.4, bf16[128,128]{1,0:T(8,128)(2,1)} %weight_h.1, f32[1,128]{1,0:T(1,128)} %bitcast.5, bf16[1024,8192]{1,0:T(8,128)(2,1)} %stripe.1, ...), custom_call_target="tpu_custom_call" | custom-call | tf_op jit(solution)/shard_map/pallas_call | solution.py:577
  39.3 1.9 %shard_map.121 = (bf16[1024,128]{1,0:T(8,128)(2,1)}, bf16[1024,128]{1,0:T(8,128)(2,1)}, f32[128,128]{1,0:T(8,128)}, f32[1,128]{1,0:T(1,128)}) custom-call(bf16[1024,128]{1,0:T(8,128)(2,1)} %get-tuple-element.12.refs_0_, bf16[1024,128]{1,0:T(8,128)(2,1)} %get-tuple-element.13.refs_1_, f32[128,128]{1,0:T(8,128)} %get-tuple-element.14.refs_2_, ...), custom_call_target="tpu_custom_call" | custom-call | tf_op jit(solution)/shard_map/pallas_call | solution.py:632

commit v3 on v2

--- a/solution.py
+++ b/solution.py
@@ -243,7 +243,7 @@
     def same(row, j):
         return meta_s[row, j].astype(F32)
 
-    unroll = 4
+    unroll = 16
 
     def scan_loop(n, row, term):
         def step(i):

time: 41.3 us -> 39.9 us (0.966)
  Pallas kernels: 40.5 us -> 39.1 us
    pallas_call x1, Pallas kernels: 38.7 us -> 37.2 us  [body(): pl.pallas_call(functools.partial(kernel, nrow, ncol, scale), out_shape=sh...]
where the time goes in v3:
time: 39.9 us; the launch traced here: 39.8 us
  Pallas kernels  39.1 us (98%)
  between operations  0.64 us (2%)
    pallas_call x1, Pallas kernels, body(): pl.pallas_call(functools.partial(kernel, nrow, ncol, scale), out_shape=sh...  37.2 us
    pallas_call x1, Pallas kernels, body(): pl.pallas_call(hand_over, out_shape=shapes, in_specs=[vmem] * 4, out_spec...  1.87 us

profile of v3, /device:TPU:1, one launch (start us, length us, event | category | flops | bytes accessed | tf_op | source)
XLA Modules:
  0.0 39.8 jit_solution(12550784426483131479)
XLA Ops:
  0.6 37.2 %shard_map.120 = (bf16[1024,128]{1,0:T(8,128)(2,1)}, bf16[1024,128]{1,0:T(8,128)(2,1)}, f32[128,128]{1,0:T(8,128)}, f32[1,128]{1,0:T(1,128)}) custom-call(bf16[8,128,128]{2,1,0:T(8,128)(2,1)} %bitcast.4, bf16[128,128]{1,0:T(8,128)(2,1)} %weight_h.1, f32[1,128]{1,0:T(1,128)} %bitcast.5, bf16[1024,8192]{1,0:T(8,128)(2,1)} %stripe.1, ...), custom_call_target="tpu_custom_call" | custom-call | tf_op jit(solution)/shard_map/pallas_call | solution.py:577
  37.9 1.9 %shard_map.121 = (bf16[1024,128]{1,0:T(8,128)(2,1)}, bf16[1024,128]{1,0:T(8,128)(2,1)}, f32[128,128]{1,0:T(8,128)}, f32[1,128]{1,0:T(1,128)}) custom-call(bf16[1024,128]{1,0:T(8,128)(2,1)} %get-tuple-element.12.refs_0_, bf16[1024,128]{1,0:T(8,128)(2,1)} %get-tuple-element.13.refs_1_, f32[128,128]{1,0:T(8,128)} %get-tuple-element.14.refs_2_, ...), custom_call_target="tpu_custom_call" | custom-call | tf_op jit(solution)/shard_map/pallas_call | solution.py:632
